TPU v7x, 32 devices: a whole 2x2x4 slice. The times are simulated.
32 devices in a mesh: sec: 2 (over y), ty: 16 (over z, x, core).
Axes of the slice: x: 2, y: 2, z: 4, core: 2. Of those that a mesh axis runs over, the one named last changes fastest.
Arguments:
- points: float32 [4, 32768], P(None, ('sec', 'ty')), parts along dimension 1, may hold values from -88 to 2136, as said below
- source: bfloat16 [1024, 2048], P(('sec', 'ty')), parts along dimension 0, may hold values from -4 to 4
- slab_first: int32 [32], P(('sec', 'ty')), parts along dimension 0, may hold values from 0 to 29, as said below
- slab_count: int32 [32], P(('sec', 'ty')), parts along dimension 0, may hold values from 3 to 6, as said below
Outputs:
- rendered: bfloat16 [1024, 2048], P(('sec', 'ty')), parts along dimension 0
- vertex_affines: float32 [6, 128, 256], P(None, ('sec', 'ty')), parts along dimension 1
There are 2 independent parts, one for each index of `sec`. A program takes and returns all parts, laid end to end along the dimension named above; each array names one. Nothing has to cross between parts.
Inputs may be any that keep to these rules, and one draw needn't show every extreme that they name: `points`: for tile t, rows 0 and 1 are fixed positions: each 16 x 16 pixel cell of rows t*32 to (t+1)*32 and columns 0 to 2048 holds 4 of them, listed cell by cell, cells in row-major order; rows 2 and 3 are the matching moving positions. Source block j is rows j*16 to (j+1)*16 - 1. Tile t samples blocks slab_first[t] to slab_first[t] + slab_count[t] - 1, all within rows (t-1)*32 to (t+2)*32 - 1. slab_count reaches 6 on some tile in every draw.
All inputs are finite; a program needn't handle non-finite values.
Results may differ from a plain program's by a relative error of at most 0.008.
Values may be sent and summed in bfloat16 or wider, within the bound.
No kernel may reach another device: no remote copies, remote signals or barrier semaphores. Data moves between devices by JAX's collectives and lax.ppermute only.
A program may use at most 64 MiB of HBM per device.

v0:
```python
import jax
import jax.numpy as jnp
from jax import lax
from jax.sharding import PartitionSpec as P

W = 2048
BH = 16
PC = 4
SP = 8
H = 32
K = 6
VR = 4
VC = 256


PRECISE = lax.Precision.HIGHEST
RIDGE_TERM = 0.01


def with_halo(block, sides, width):
    for axis, dim in sides:
        count = lax.axis_size(axis)
        forward = [(i, i + 1) for i in range(count - 1)]
        backward = [(target, source) for source, target in forward]
        low = lax.ppermute(
            lax.slice_in_dim(block, block.shape[dim] - width, None, axis=dim), axis, forward
        )
        high = lax.ppermute(lax.slice_in_dim(block, 0, width, axis=dim), axis, backward)
        block = jnp.concatenate([low, block, high], axis=dim)
    return block


def solve_affine(moments, vertex_x, vertex_y):
    mass = moments[0]
    mean_px = moments[1] / mass
    mean_py = moments[2] / mass
    mean_qx = moments[3] / mass
    mean_qy = moments[4] / mass
    cov_xx = moments[5] / mass - mean_px * mean_px + RIDGE_TERM
    cov_xy = moments[6] / mass - mean_px * mean_py
    cov_yy = moments[7] / mass - mean_py * mean_py + RIDGE_TERM
    cross_xx = moments[8] / mass - mean_qx * mean_px
    cross_xy = moments[9] / mass - mean_qx * mean_py
    cross_yx = moments[10] / mass - mean_qy * mean_px
    cross_yy = moments[11] / mass - mean_qy * mean_py
    determ = cov_xx * cov_yy - cov_xy * cov_xy
    lin_xx = (cross_xx * cov_yy - cross_xy * cov_xy) / determ
    lin_xy = (cross_xy * cov_xx - cross_xx * cov_xy) / determ
    lin_yx = (cross_yx * cov_yy - cross_yy * cov_xy) / determ
    lin_yy = (cross_yy * cov_xx - cross_yx * cov_xy) / determ
    delta_x = vertex_x - mean_px
    delta_y = vertex_y - mean_py
    shift_x = mean_qx + lin_xx * delta_x + lin_xy * delta_y - vertex_x
    shift_y = mean_qy + lin_yx * delta_x + lin_yy * delta_y - vertex_y
    return jnp.stack([lin_xx, lin_xy, lin_yx, lin_yy, shift_x, shift_y])


def block_moments(pts, usable, strip_id):
    block_count = W // 128
    per_block = VC // block_count
    cell_rows = pts.shape[1] // (block_count * 8 * PC)
    grid = pts.reshape(4, cell_rows, block_count, 8 * PC)
    live = usable.reshape(cell_rows, block_count, 8 * PC)
    grid = jnp.pad(grid, ((0, 0), (0, 0), (1, 1), (0, 0)))
    live = jnp.pad(live, ((0, 0), (1, 1), (0, 0)))
    near = jnp.concatenate(
        [
            grid[:, :, 0:block_count],
            grid[:, :, 1 : block_count + 1],
            grid[:, :, 2 : block_count + 2],
        ],
        axis=3,
    )
    near_live = jnp.concatenate(
        [live[:, 0:block_count], live[:, 1 : block_count + 1], live[:, 2 : block_count + 2]], axis=2
    )
    near = jnp.transpose(near, (0, 2, 1, 3)).reshape(4, block_count, cell_rows * 24 * PC)
    near_live = jnp.transpose(near_live, (1, 0, 2)).reshape(block_count, cell_rows * 24 * PC)
    centre_y = strip_id.astype(jnp.float32) * H + H / 2.0
    anchor = jnp.arange(block_count, dtype=jnp.float32) * 128.0 + 64.0
    fixed_x = (near[0] - anchor[:, None]) / H
    fixed_y = (near[1] - centre_y) / H
    moved_x = (near[2] - anchor[:, None]) / H
    moved_y = (near[3] - centre_y) / H
    unit_row = jnp.ones_like(fixed_x)
    features = (
        jnp.stack(
            [
                unit_row,
                fixed_x,
                fixed_y,
                moved_x,
                moved_y,
                fixed_x * fixed_x,
                fixed_x * fixed_y,
                fixed_y * fixed_y,
                moved_x * fixed_x,
                moved_x * fixed_y,
                moved_y * fixed_x,
                moved_y * fixed_y,
            ],
            axis=1,
        )
        * near_live[:, None, :]
    )
    vertex_col = jnp.arange(VC, dtype=jnp.float32).reshape(block_count, per_block) * SP + SP / 2.0
    vertex_row = jnp.arange(VR, dtype=jnp.float32) * SP + SP / 2.0 - H / 2.0
    gap_x = (near[0][:, :, None] - vertex_col[:, None, :]) / H
    gap_y = fixed_y[:, :, None] - (vertex_row / H)[None, None, :]
    weight_x = jnp.exp(-2.0 * gap_x * gap_x)
    weight_y = jnp.exp(-2.0 * gap_y * gap_y)
    weighted = features[:, :, None, :] * jnp.transpose(weight_y, (0, 2, 1))[:, None, :, :]
    moments = jnp.einsum("bkrm,bmc->bkrc", weighted, weight_x, precision=PRECISE)
    return jnp.transpose(moments, (1, 2, 0, 3)).reshape(12, VR, VC)


def vertex_frame():
    block_count = W // 128
    per_block = VC // block_count
    anchor = jnp.arange(block_count, dtype=jnp.float32) * 128.0 + 64.0
    vertex_col = jnp.arange(VC, dtype=jnp.float32) * SP + SP / 2.0
    vertex_row = jnp.arange(VR, dtype=jnp.float32) * SP + SP / 2.0 - H / 2.0
    column_anchor = jnp.repeat(anchor, per_block)
    vertex_x = jnp.broadcast_to(((vertex_col - column_anchor) / H)[None, :], (VR, VC))
    vertex_y = jnp.broadcast_to((vertex_row / H)[:, None], (VR, VC))
    return (vertex_x, vertex_y)


def tent_tables():
    row_local = jnp.arange(H, dtype=jnp.float32)
    ext_row = (jnp.arange(VR + 2, dtype=jnp.float32) - 1.0) * SP + SP / 2.0
    tent_rows = jnp.maximum(0.0, 1.0 - jnp.abs(row_local[:, None] - ext_row[None, :]) / SP)
    column = jnp.clip(jnp.arange(W, dtype=jnp.float32), SP / 2.0, W - SP / 2.0)
    vertex_col = jnp.arange(VC, dtype=jnp.float32) * SP + SP / 2.0
    tent_cols = jnp.maximum(0.0, 1.0 - jnp.abs(column[None, :] - vertex_col[:, None]) / SP)
    return (tent_rows, tent_cols)


def displace(near_shift, tent_rows, tent_cols):
    first_part = jnp.dot(
        jnp.dot(tent_rows, near_shift[0], precision=PRECISE), tent_cols, precision=PRECISE
    )
    second_part = jnp.dot(
        jnp.dot(tent_rows, near_shift[1], precision=PRECISE), tent_cols, precision=PRECISE
    )
    return jnp.stack([first_part, second_part])


def render_strip(slab_rows, first_slab, slab_total, disp, strip_id):
    block_count = W // 128
    samp_y = jnp.arange(H, dtype=jnp.float32)[:, None] + H * disp[1]
    samp_x = jnp.arange(W, dtype=jnp.float32)[None, :] + H * disp[0]
    slot_ids = jnp.arange(K, dtype=jnp.int32)
    slot_row = (first_slab + slot_ids) * BH - strip_id * H
    row_pos = (
        (slot_row[:, None] + jnp.arange(BH, dtype=jnp.int32)[None, :])
        .reshape(K * BH)
        .astype(jnp.float32)
    )
    slot_live = jnp.repeat((slot_ids < slab_total).astype(jnp.float32), BH)
    padded = jnp.pad(slab_rows, ((0, 0), (64, 192)))
    blocks = padded.reshape(K * BH, block_count + 2, 128)
    windows = jnp.concatenate([blocks[:, :block_count], blocks[:, 1 : block_count + 1]], axis=2)
    windows = jnp.transpose(windows, (1, 0, 2))
    block_y = samp_y.reshape(H, block_count, 128).transpose(1, 0, 2).reshape(block_count, H * 128)
    block_x = samp_x.reshape(H, block_count, 128).transpose(1, 0, 2).reshape(block_count, H * 128)
    block_ids = jnp.arange(block_count, dtype=jnp.int32)

    def one_block(packed):
        along_y, along_x, window, block_id = packed
        col_pos = block_id.astype(jnp.float32) * 128.0 - 64.0 + jnp.arange(256, dtype=jnp.float32)
        across = jnp.maximum(0.0, 1.0 - jnp.abs(along_x[:, None] - col_pos[None, :])).astype(
            jnp.bfloat16
        )
        mixed_rows = lax.dot_general(
            across, window, (((1,), (1,)), ((), ())), preferred_element_type=jnp.float32
        )
        tent_y = jnp.maximum(0.0, 1.0 - jnp.abs(along_y[:, None] - row_pos[None, :])) * slot_live
        return jnp.sum(mixed_rows * tent_y, axis=1)

    pieces = lax.map(one_block, (block_y, block_x, windows, block_ids))
    return pieces.reshape(block_count, H, 128).transpose(1, 0, 2).reshape(H, W).astype(jnp.bfloat16)


def per_device(points, source, slab_first, slab_count):
    strip_id = lax.axis_index("ty")
    strip_span = lax.axis_size("ty")
    tile_len = points.shape[1]
    vertex_x, vertex_y = vertex_frame()
    nearby = with_halo(points, (("ty", 1),), tile_len)
    owners = strip_id - 1 + jnp.arange(3 * tile_len, dtype=jnp.int32) // tile_len
    usable = ((owners >= 0) & (owners < strip_span)).astype(jnp.float32)
    moments = block_moments(nearby, usable, strip_id)
    affines = solve_affine(moments, vertex_x, vertex_y)
    own_shift = affines[4:6]
    extended = with_halo(own_shift, (("ty", 1),), 1)
    upper_row = jnp.where(strip_id == 0, own_shift[:, :1], extended[:, :1])
    lower_row = jnp.where(strip_id == strip_span - 1, own_shift[:, -1:], extended[:, -1:])
    near_shift = jnp.concatenate([upper_row, own_shift, lower_row], axis=1)
    first_slab = slab_first[0]
    slab_total = slab_count[0]
    slot_rows = ((first_slab + jnp.arange(K, dtype=jnp.int32)) * BH)[:, None] + jnp.arange(
        BH, dtype=jnp.int32
    )[None, :]
    slot_rows = slot_rows.reshape(K * BH)
    wider = with_halo(source, (("ty", 0),), H)
    local_row = jnp.clip(slot_rows - (strip_id * H - H), 0, wider.shape[0] - 1)
    slab_rows = jnp.take(wider, local_row, axis=0)
    tent_rows, tent_cols = tent_tables()
    disp = displace(near_shift, tent_rows, tent_cols)
    rendered = render_strip(slab_rows, first_slab, slab_total, disp, strip_id)
    return (rendered, affines)


def solution(mesh):
    return jax.shard_map(
        per_device,
        mesh=mesh,
        in_specs=(
            P(None, ("sec", "ty")),
            P(("sec", "ty"), None),
            P(("sec", "ty")),
            P(("sec", "ty")),
        ),
        out_specs=(P(("sec", "ty"), None), P(None, ("sec", "ty"), None)),
        check_vma=False,
    )
```

profile of v0, /device:TPU:7, one launch (start us, length us, event | category | flops | bytes accessed | tf_op | source)
XLA Modules:
  0.0 89.9 jit_solution(14883813862441094956)
XLA Ops:
  0.6 3.7 %collective-permute-start = (f32[4,1024]{1,0:T(4,128)}, f32[4,1024]{1,0:T(4,128)S(1)}, u32[]{:S(2)}, u32[]{:S(2)}) collective-permute-start(f32[4,1024]{1,0:T(4,128)} %param.6), channel_id=1, source_target_pairs={{0,1},{1,2},{2,3},{3,4},{4,5},{5,6},{6,7},{7,8},{8,9},{9,10},{10,1... | collective-permute-start | bytes 49160 | tf_op jit(solution)/shard_map/ppermute | solution.py:25
  4.4 1.9 %collective-permute-start.1 = (f32[4,1024]{1,0:T(4,128)}, f32[4,1024]{1,0:T(4,128)S(1)}, u32[]{:S(2)}, u32[]{:S(2)}) collective-permute-start(f32[4,1024]{1,0:T(4,128)} %param.6), channel_id=1, source_target_pairs={{1,0},{2,1},{3,2},{4,3},{5,4},{6,5},{7,6},{8,7},{9,8},{10,9},{11,1... | collective-permute-start | bytes 49160 | tf_op jit(solution)/shard_map/ppermute | solution.py:28
  6.3 4.5 %collective-permute-start.4 = (bf16[32,2048]{1,0:T(8,128)(2,1)}, bf16[32,2048]{1,0:T(8,128)(2,1)S(1)}, u32[]{:S(2)}, u32[]{:S(2)}) collective-permute-start(bf16[32,2048]{1,0:T(8,128)(2,1)} %param.7), channel_id=1, source_target_pairs={{0,1},{1,2},{2,3},{3,4},{4,5},{5,6},{6,7},{7,8},{8,9},{9,10},{10,1... | collective-permute-start | bytes 393224 | tf_op jit(solution)/shard_map/ppermute | solution.py:25
  10.9 1.9 %collective-permute-start.5 = (bf16[32,2048]{1,0:T(8,128)(2,1)}, bf16[32,2048]{1,0:T(8,128)(2,1)S(1)}, u32[]{:S(2)}, u32[]{:S(2)}) collective-permute-start(bf16[32,2048]{1,0:T(8,128)(2,1)} %param.7), channel_id=1, source_target_pairs={{1,0},{2,1},{3,2},{4,3},{5,4},{6,5},{7,6},{8,7},{9,8},{10,9},{11,1... | collective-permute-start | bytes 393224 | tf_op jit(solution)/shard_map/ppermute | solution.py:28
  14.3 0.7 pad_maximum_fusion.1
  16.9 2.7 %fusion.20 = f32[12,4,16,16]{3,0,1,2:T(8,128)S(1)} fusion(f32[16,4,576]{2,1,0:T(4,128)S(1)} %fusion.43, f32[16,12,576]{2,1,0:T(8,128)S(1)} %copy.13, f32[16,16]{1,0:T(8,128)S(1)} %multiply_add_fusion.1, f32[16,576]{1,0:T(8,128)S(1)} %sub.678), kind=kOutput, calls=%fused_computation.28 | convolution fusion | flops 85966848 | bytes 676864 | tf_op jit(solution)/shard_map/bkrm,bmc->bkrc/dot_general | solution.py:113
  21.2 4.5 %collective-permute-start.2 = (f32[2,1,256]{2,1,0:T(1,128)S(1)}, f32[2,1,256]{2,1,0:T(1,128)S(1)}, u32[]{:S(2)}, u32[]{:S(2)}) collective-permute-start(f32[2,1,256]{2,1,0:T(1,128)S(1)} %pad_maximum_fusion.3), channel_id=1, source_target_pairs={{0,1},{1,2},{2,3},{3,4},{4,5},{5,6},{6,7},{7,8},{8,9},{9,10},{10,1... | collective-permute-start | bytes 6152 | tf_op jit(solution)/shard_map/ppermute | solution.py:25
  26.4 1.9 %collective-permute-start.3 = (f32[2,1,256]{2,1,0:T(1,128)S(1)}, f32[2,1,256]{2,1,0:T(1,128)S(1)}, u32[]{:S(2)}, u32[]{:S(2)}) collective-permute-start(f32[2,1,256]{2,1,0:T(1,128)S(1)} %get-tuple-element.165), channel_id=1, source_target_pairs={{1,0},{2,1},{3,2},{4,3},{5,4},{6,5},{7,6},{8,7},{9,8},{10,9},{11,1... | collective-permute-start | bytes 6152 | tf_op jit(solution)/shard_map/ppermute | solution.py:28
  28.4 4.4 %collective-permute-done.3 = f32[2,1,256]{2,1,0:T(1,128)S(1)} collective-permute-done((f32[2,1,256]{2,1,0:T(1,128)S(1)}, f32[2,1,256]{2,1,0:T(1,128)S(1)}, u32[]{:S(2)}, u32[]{:S(2)}) %collective-permute-start.3) | collective-permute-done | bytes 2080 | tf_op jit(solution)/shard_map/ppermute | solution.py:28
  33.1 1.7 %fusion.23 = f32[4,8,16,128]{3,1,2,0:T(8,128)S(1)} fusion(f32[32,256]{1,0:T(8,128)S(1)} %fusion.51, f32[256]{0:T(256)S(1)} %multiply_add_fusion.2, f32[2048]{0:T(1024)S(1)} %iota_clamp_fusion), kind=kOutput, calls=%fused_computation.29 | convolution fusion | flops 204079104 | bytes 304128 | tf_op jit(solution)/shard_map/dot_general | solution.py:140
  34.9 1.7 %fusion.24 = f32[4,8,16,128]{3,1,2,0:T(8,128)S(1)} fusion(f32[32,256]{1,0:T(8,128)S(1)} %fusion.50, f32[256]{0:T(256)S(1)} %multiply_add_fusion.2, f32[2048]{0:T(1024)S(1)} %iota_clamp_fusion), kind=kOutput, calls=%fused_computation.30 | convolution fusion | flops 204079104 | bytes 304128 | tf_op jit(solution)/shard_map/dot_general | solution.py:143
  36.7 0.8 copy-done
  37.5 0.8 gather_fusion
  39.2 0.2 copy.27
  39.5 49.7 %while.13 = (s32[]{:T(128)}, bf16[16,4096]{1,0:T(8,128)(2,1)S(1)}, f32[16,4096]{1,0:T(8,128)S(1)}, s32[16]{0:T(128)S(1)}, bf16[16,96,256]{2,1,0:T(8,128)(2,1)S(1...) while((s32[]{:T(128)}, bf16[16,4096]{1,0:T(8,128)(2,1)S(1)}, ...), condition=%wide.region_2.3_spmd.clone, body=%wide.region_0.2_spmd.clone.sunk | while | flops 209318336 | bytes 202209 | solution.py:181
  39.5 0.6 dynamic_slice.42
  41.1 1.3 %fusion.82 = f32[4096]{0:T(1024)S(1)} fusion(f32[256]{0:T(256)S(1)} %iota_add_fusion.2, f32[4096]{0:T(1024)S(1)} %bitcast.100, f32[96]{0:T(128)S(1)} %mul.863, f32[96]{0:T(128)S(1)} %convert_element_type.81, f32[4096]{0:T(1024)S(1)} %bitcast.99, bf16[16,96,256]{2,1,0:T(8,128)(2,1)S(1)} %get-tuple-element.272, s32[]{:T(128)} %get-tuple-element.256), kind=kOutput, calls=%fused_computation.9.clone.1 | convolution fusion | flops 209317888 | bytes 100356 | tf_op jit(solution)/shard_map/while/body/eval_jaxpr/dot_general | solution.py:175
  42.6 0.6 dynamic_slice.42
  44.2 1.3 %fusion.82 = f32[4096]{0:T(1024)S(1)} fusion(f32[256]{0:T(256)S(1)} %iota_add_fusion.2, f32[4096]{0:T(1024)S(1)} %bitcast.100, f32[96]{0:T(128)S(1)} %mul.863, f32[96]{0:T(128)S(1)} %convert_element_type.81, f32[4096]{0:T(1024)S(1)} %bitcast.99, bf16[16,96,256]{2,1,0:T(8,128)(2,1)S(1)} %get-tuple-element.272, s32[]{:T(128)} %get-tuple-element.256), kind=kOutput, calls=%fused_computation.9.clone.1 | convolution fusion | flops 209317888 | bytes 100356 | tf_op jit(solution)/shard_map/while/body/eval_jaxpr/dot_general | solution.py:175
  45.7 0.6 dynamic_slice.42
  47.3 1.3 %fusion.82 = f32[4096]{0:T(1024)S(1)} fusion(f32[256]{0:T(256)S(1)} %iota_add_fusion.2, f32[4096]{0:T(1024)S(1)} %bitcast.100, f32[96]{0:T(128)S(1)} %mul.863, f32[96]{0:T(128)S(1)} %convert_element_type.81, f32[4096]{0:T(1024)S(1)} %bitcast.99, bf16[16,96,256]{2,1,0:T(8,128)(2,1)S(1)} %get-tuple-element.272, s32[]{:T(128)} %get-tuple-element.256), kind=kOutput, calls=%fused_computation.9.clone.1 | convolution fusion | flops 209317888 | bytes 100356 | tf_op jit(solution)/shard_map/while/body/eval_jaxpr/dot_general | solution.py:175
  48.8 0.6 dynamic_slice.42
  50.4 1.3 %fusion.82 = f32[4096]{0:T(1024)S(1)} fusion(f32[256]{0:T(256)S(1)} %iota_add_fusion.2, f32[4096]{0:T(1024)S(1)} %bitcast.100, f32[96]{0:T(128)S(1)} %mul.863, f32[96]{0:T(128)S(1)} %convert_element_type.81, f32[4096]{0:T(1024)S(1)} %bitcast.99, bf16[16,96,256]{2,1,0:T(8,128)(2,1)S(1)} %get-tuple-element.272, s32[]{:T(128)} %get-tuple-element.256), kind=kOutput, calls=%fused_computation.9.clone.1 | convolution fusion | flops 209317888 | bytes 100356 | tf_op jit(solution)/shard_map/while/body/eval_jaxpr/dot_general | solution.py:175
  51.9 0.6 dynamic_slice.42
  53.5 1.3 %fusion.82 = f32[4096]{0:T(1024)S(1)} fusion(f32[256]{0:T(256)S(1)} %iota_add_fusion.2, f32[4096]{0:T(1024)S(1)} %bitcast.100, f32[96]{0:T(128)S(1)} %mul.863, f32[96]{0:T(128)S(1)} %convert_element_type.81, f32[4096]{0:T(1024)S(1)} %bitcast.99, bf16[16,96,256]{2,1,0:T(8,128)(2,1)S(1)} %get-tuple-element.272, s32[]{:T(128)} %get-tuple-element.256), kind=kOutput, calls=%fused_computation.9.clone.1 | convolution fusion | flops 209317888 | bytes 100356 | tf_op jit(solution)/shard_map/while/body/eval_jaxpr/dot_general | solution.py:175
  55.0 0.6 dynamic_slice.42
  56.6 1.3 %fusion.82 = f32[4096]{0:T(1024)S(1)} fusion(f32[256]{0:T(256)S(1)} %iota_add_fusion.2, f32[4096]{0:T(1024)S(1)} %bitcast.100, f32[96]{0:T(128)S(1)} %mul.863, f32[96]{0:T(128)S(1)} %convert_element_type.81, f32[4096]{0:T(1024)S(1)} %bitcast.99, bf16[16,96,256]{2,1,0:T(8,128)(2,1)S(1)} %get-tuple-element.272, s32[]{:T(128)} %get-tuple-element.256), kind=kOutput, calls=%fused_computation.9.clone.1 | convolution fusion | flops 209317888 | bytes 100356 | tf_op jit(solution)/shard_map/while/body/eval_jaxpr/dot_general | solution.py:175
  58.1 0.6 dynamic_slice.42
  59.7 1.3 %fusion.82 = f32[4096]{0:T(1024)S(1)} fusion(f32[256]{0:T(256)S(1)} %iota_add_fusion.2, f32[4096]{0:T(1024)S(1)} %bitcast.100, f32[96]{0:T(128)S(1)} %mul.863, f32[96]{0:T(128)S(1)} %convert_element_type.81, f32[4096]{0:T(1024)S(1)} %bitcast.99, bf16[16,96,256]{2,1,0:T(8,128)(2,1)S(1)} %get-tuple-element.272, s32[]{:T(128)} %get-tuple-element.256), kind=kOutput, calls=%fused_computation.9.clone.1 | convolution fusion | flops 209317888 | bytes 100356 | tf_op jit(solution)/shard_map/while/body/eval_jaxpr/dot_general | solution.py:175
  61.2 0.6 dynamic_slice.42
  62.8 1.3 %fusion.82 = f32[4096]{0:T(1024)S(1)} fusion(f32[256]{0:T(256)S(1)} %iota_add_fusion.2, f32[4096]{0:T(1024)S(1)} %bitcast.100, f32[96]{0:T(128)S(1)} %mul.863, f32[96]{0:T(128)S(1)} %convert_element_type.81, f32[4096]{0:T(1024)S(1)} %bitcast.99, bf16[16,96,256]{2,1,0:T(8,128)(2,1)S(1)} %get-tuple-element.272, s32[]{:T(128)} %get-tuple-element.256), kind=kOutput, calls=%fused_computation.9.clone.1 | convolution fusion | flops 209317888 | bytes 100356 | tf_op jit(solution)/shard_map/while/body/eval_jaxpr/dot_general | solution.py:175
  64.3 0.6 dynamic_slice.42
  65.9 1.3 %fusion.82 = f32[4096]{0:T(1024)S(1)} fusion(f32[256]{0:T(256)S(1)} %iota_add_fusion.2, f32[4096]{0:T(1024)S(1)} %bitcast.100, f32[96]{0:T(128)S(1)} %mul.863, f32[96]{0:T(128)S(1)} %convert_element_type.81, f32[4096]{0:T(1024)S(1)} %bitcast.99, bf16[16,96,256]{2,1,0:T(8,128)(2,1)S(1)} %get-tuple-element.272, s32[]{:T(128)} %get-tuple-element.256), kind=kOutput, calls=%fused_computation.9.clone.1 | convolution fusion | flops 209317888 | bytes 100356 | tf_op jit(solution)/shard_map/while/body/eval_jaxpr/dot_general | solution.py:175
  67.5 0.6 dynamic_slice.42
  69.0 1.3 %fusion.82 = f32[4096]{0:T(1024)S(1)} fusion(f32[256]{0:T(256)S(1)} %iota_add_fusion.2, f32[4096]{0:T(1024)S(1)} %bitcast.100, f32[96]{0:T(128)S(1)} %mul.863, f32[96]{0:T(128)S(1)} %convert_element_type.81, f32[4096]{0:T(1024)S(1)} %bitcast.99, bf16[16,96,256]{2,1,0:T(8,128)(2,1)S(1)} %get-tuple-element.272, s32[]{:T(128)} %get-tuple-element.256), kind=kOutput, calls=%fused_computation.9.clone.1 | convolution fusion | flops 209317888 | bytes 100356 | tf_op jit(solution)/shard_map/while/body/eval_jaxpr/dot_general | solution.py:175
  70.6 0.6 dynamic_slice.42
  72.1 1.3 %fusion.82 = f32[4096]{0:T(1024)S(1)} fusion(f32[256]{0:T(256)S(1)} %iota_add_fusion.2, f32[4096]{0:T(1024)S(1)} %bitcast.100, f32[96]{0:T(128)S(1)} %mul.863, f32[96]{0:T(128)S(1)} %convert_element_type.81, f32[4096]{0:T(1024)S(1)} %bitcast.99, bf16[16,96,256]{2,1,0:T(8,128)(2,1)S(1)} %get-tuple-element.272, s32[]{:T(128)} %get-tuple-element.256), kind=kOutput, calls=%fused_computation.9.clone.1 | convolution fusion | flops 209317888 | bytes 100356 | tf_op jit(solution)/shard_map/while/body/eval_jaxpr/dot_general | solution.py:175
  73.7 0.6 dynamic_slice.42
  75.2 1.3 %fusion.82 = f32[4096]{0:T(1024)S(1)} fusion(f32[256]{0:T(256)S(1)} %iota_add_fusion.2, f32[4096]{0:T(1024)S(1)} %bitcast.100, f32[96]{0:T(128)S(1)} %mul.863, f32[96]{0:T(128)S(1)} %convert_element_type.81, f32[4096]{0:T(1024)S(1)} %bitcast.99, bf16[16,96,256]{2,1,0:T(8,128)(2,1)S(1)} %get-tuple-element.272, s32[]{:T(128)} %get-tuple-element.256), kind=kOutput, calls=%fused_computation.9.clone.1 | convolution fusion | flops 209317888 | bytes 100356 | tf_op jit(solution)/shard_map/while/body/eval_jaxpr/dot_general | solution.py:175
  76.8 0.6 dynamic_slice.42
  78.3 1.3 %fusion.82 = f32[4096]{0:T(1024)S(1)} fusion(f32[256]{0:T(256)S(1)} %iota_add_fusion.2, f32[4096]{0:T(1024)S(1)} %bitcast.100, f32[96]{0:T(128)S(1)} %mul.863, f32[96]{0:T(128)S(1)} %convert_element_type.81, f32[4096]{0:T(1024)S(1)} %bitcast.99, bf16[16,96,256]{2,1,0:T(8,128)(2,1)S(1)} %get-tuple-element.272, s32[]{:T(128)} %get-tuple-element.256), kind=kOutput, calls=%fused_computation.9.clone.1 | convolution fusion | flops 209317888 | bytes 100356 | tf_op jit(solution)/shard_map/while/body/eval_jaxpr/dot_general | solution.py:175
  79.9 0.6 dynamic_slice.42
  81.4 1.3 %fusion.82 = f32[4096]{0:T(1024)S(1)} fusion(f32[256]{0:T(256)S(1)} %iota_add_fusion.2, f32[4096]{0:T(1024)S(1)} %bitcast.100, f32[96]{0:T(128)S(1)} %mul.863, f32[96]{0:T(128)S(1)} %convert_element_type.81, f32[4096]{0:T(1024)S(1)} %bitcast.99, bf16[16,96,256]{2,1,0:T(8,128)(2,1)S(1)} %get-tuple-element.272, s32[]{:T(128)} %get-tuple-element.256), kind=kOutput, calls=%fused_computation.9.clone.1 | convolution fusion | flops 209317888 | bytes 100356 | tf_op jit(solution)/shard_map/while/body/eval_jaxpr/dot_general | solution.py:175
  83.0 0.6 dynamic_slice.42
  84.5 1.3 %fusion.82 = f32[4096]{0:T(1024)S(1)} fusion(f32[256]{0:T(256)S(1)} %iota_add_fusion.2, f32[4096]{0:T(1024)S(1)} %bitcast.100, f32[96]{0:T(128)S(1)} %mul.863, f32[96]{0:T(128)S(1)} %convert_element_type.81, f32[4096]{0:T(1024)S(1)} %bitcast.99, bf16[16,96,256]{2,1,0:T(8,128)(2,1)S(1)} %get-tuple-element.272, s32[]{:T(128)} %get-tuple-element.256), kind=kOutput, calls=%fused_computation.9.clone.1 | convolution fusion | flops 209317888 | bytes 100356 | tf_op jit(solution)/shard_map/while/body/eval_jaxpr/dot_general | solution.py:175
  86.1 0.6 dynamic_slice.42
  87.6 1.3 %fusion.82 = f32[4096]{0:T(1024)S(1)} fusion(f32[256]{0:T(256)S(1)} %iota_add_fusion.2, f32[4096]{0:T(1024)S(1)} %bitcast.100, f32[96]{0:T(128)S(1)} %mul.863, f32[96]{0:T(128)S(1)} %convert_element_type.81, f32[4096]{0:T(1024)S(1)} %bitcast.99, bf16[16,96,256]{2,1,0:T(8,128)(2,1)S(1)} %get-tuple-element.272, s32[]{:T(128)} %get-tuple-element.256), kind=kOutput, calls=%fused_computation.9.clone.1 | convolution fusion | flops 209317888 | bytes 100356 | tf_op jit(solution)/shard_map/while/body/eval_jaxpr/dot_general | solution.py:175
  89.2 0.7 copy.40
  (216 shorter events, 14.6 us)
Async XLA Ops:
  0.6 13.6 %collective-permute-start = (f32[4,1024]{1,0:T(4,128)}, f32[4,1024]{1,0:T(4,128)S(1)}, u32[]{:S(2)}, u32[]{:S(2)}) collective-permute-start(f32[4,1024]{1,0:T(4,128)} %param.6), channel_id=1, source_target_pairs={{0,1},{1,2},{2,3},{3,4},{4,5},{5,6},{6,7},{7,8},{8,9},{9,10},{10,1... | collective-permute-start | bytes 49160 | tf_op jit(solution)/shard_map/ppermute | solution.py:25
  4.4 9.9 %collective-permute-start.1 = (f32[4,1024]{1,0:T(4,128)}, f32[4,1024]{1,0:T(4,128)S(1)}, u32[]{:S(2)}, u32[]{:S(2)}) collective-permute-start(f32[4,1024]{1,0:T(4,128)} %param.6), channel_id=1, source_target_pairs={{1,0},{2,1},{3,2},{4,3},{5,4},{6,5},{7,6},{8,7},{9,8},{10,9},{11,1... | collective-permute-start | bytes 49160 | tf_op jit(solution)/shard_map/ppermute | solution.py:28
  6.3 30.4 %collective-permute-start.4 = (bf16[32,2048]{1,0:T(8,128)(2,1)}, bf16[32,2048]{1,0:T(8,128)(2,1)S(1)}, u32[]{:S(2)}, u32[]{:S(2)}) collective-permute-start(bf16[32,2048]{1,0:T(8,128)(2,1)} %param.7), channel_id=1, source_target_pairs={{0,1},{1,2},{2,3},{3,4},{4,5},{5,6},{6,7},{7,8},{8,9},{9,10},{10,1... | collective-permute-start | bytes 393224 | tf_op jit(solution)/shard_map/ppermute | solution.py:25
  10.9 25.9 %collective-permute-start.5 = (bf16[32,2048]{1,0:T(8,128)(2,1)}, bf16[32,2048]{1,0:T(8,128)(2,1)S(1)}, u32[]{:S(2)}, u32[]{:S(2)}) collective-permute-start(bf16[32,2048]{1,0:T(8,128)(2,1)} %param.7), channel_id=1, source_target_pairs={{1,0},{2,1},{3,2},{4,3},{5,4},{6,5},{7,6},{8,7},{9,8},{10,9},{11,1... | collective-permute-start | bytes 393224 | tf_op jit(solution)/shard_map/ppermute | solution.py:28
  21.2 13.7 %copy-start.1 = (f32[6,4,256]{2,1,0:T(4,128)}, f32[6,4,256]{2,1,0:T(4,128)S(1)}, u32[]{:S(2)}) copy-start(f32[6,4,256]{2,1,0:T(4,128)S(1)} %get-tuple-element.149) | copy-start | bytes 73732
  21.2 5.3 %collective-permute-start.2 = (f32[2,1,256]{2,1,0:T(1,128)S(1)}, f32[2,1,256]{2,1,0:T(1,128)S(1)}, u32[]{:S(2)}, u32[]{:S(2)}) collective-permute-start(f32[2,1,256]{2,1,0:T(1,128)S(1)} %pad_maximum_fusion.3), channel_id=1, source_target_pairs={{0,1},{1,2},{2,3},{3,4},{4,5},{5,6},{6,7},{7,8},{8,9},{9,10},{10,1... | collective-permute-start | bytes 6152 | tf_op jit(solution)/shard_map/ppermute | solution.py:25
  26.4 6.3 %collective-permute-start.3 = (f32[2,1,256]{2,1,0:T(1,128)S(1)}, f32[2,1,256]{2,1,0:T(1,128)S(1)}, u32[]{:S(2)}, u32[]{:S(2)}) collective-permute-start(f32[2,1,256]{2,1,0:T(1,128)S(1)} %get-tuple-element.165), channel_id=1, source_target_pairs={{1,0},{2,1},{3,2},{4,3},{5,4},{6,5},{7,6},{8,7},{9,8},{10,9},{11,1... | collective-permute-start | bytes 6152 | tf_op jit(solution)/shard_map/ppermute | solution.py:28
  36.6 0.9 %copy-start = (bf16[32,2048]{1,0:T(8,128)(2,1)S(1)}, bf16[32,2048]{1,0:T(8,128)(2,1)}, u32[]{:S(2)}) copy-start(bf16[32,2048]{1,0:T(8,128)(2,1)} %param.7) | copy-start | bytes 393220
where the time goes:
time: 90.3 us; the launch traced here: 89.9 us
  matrix products  26.5 us (29%)
  local copies, waits for them, and re-layouts  23 us (25%)
  starting transfers between devices  18.6 us (21%)
  loops' own time  10.9 us (12%)
  waiting for transfers between devices  4.45 us (5%)
  other arithmetic  4.08 us (5%)
  between operations  2.41 us (3%)
    dot_general x16, matrix products, one_block(): lax.dot_general(across, window, (((1,), (1,)), ((), ())), preferred_eleme...  20.1 us
    ppermute x3, starting transfers between devices, with_halo(): lax.ppermute(lax.slice_in_dim(block, block.shape[dim] - width, None, axis...  12.8 us
    another operation x1, loops' own time, render_strip(): pieces = lax.map(one_block, (block_y, block_x, windows, block_ids))  10.9 us
    dynamic_slice x32, local copies, waits for them, and re-layouts, render_strip(): pieces = lax.map(one_block, (block_y, block_x, windows, block_ids))  10.1 us
    ppermute x3, starting transfers between devices, with_halo(): lax.ppermute(lax.slice_in_dim(block, 0, width, axis=dim), axis, backward)  5.75 us
    ppermute x3, waiting for transfers between devices, with_halo(): lax.ppermute(lax.slice_in_dim(block, 0, width, axis=dim), axis, backward)  4.4 us
    dynamic_update_slice x16, local copies, waits for them, and re-layouts, render_strip(): pieces = lax.map(one_block, (block_y, block_x, windows, block_ids))  3.62 us
    dot_general x1, matrix products, block_moments(): jnp.einsum('bkrm,bmc->bkrc', weighted, weight_x, precision=PRECISE)  2.68 us
  transfers between devices with their start and end apart: 6, of which 1 were waited for; matrix products, arithmetic and copies ran while one was open for 13% of the time, Pallas kernels for 0%

commit v1 on v0

v1 whole, which is shorter than its diff:
```python
import functools

import jax
import jax.numpy as jnp
import numpy as np
from jax import lax
from jax.experimental import pallas as pl
from jax.experimental.pallas import tpu as pltpu
from jax.sharding import PartitionSpec as P

BH = 16
PC = 4
SP = 8
VR = 4
LANES = 128
CELL = 16
RIDGE_TERM = 0.01
FEATS = 12
ER = 8
NF = FEATS * ER
GROUP_PX = LANES // PC * CELL
NV = GROUP_PX // SP + 2 * LANES // SP
EXP2_SCALE = 2.0 * float(np.log2(np.e))
TAPS = 8
TOP_PAD = 8
LOW_PAD = 16


def fiota(shape, dim):
    return lax.broadcasted_iota(jnp.int32, shape, dim).astype(jnp.float32)


def local_points(pts, tile, cell_cols, height):
    lane = lax.broadcasted_iota(jnp.int32, (1, pts.shape[1]), 1)
    cell = lane // PC
    base_x = (cell % cell_cols * CELL).astype(jnp.float32)
    base_y = (tile * height + cell // cell_cols * CELL).astype(jnp.float32)
    fixed_x, fixed_y = pts[0:1], pts[1:2]
    return jnp.concatenate(
        [fixed_x - base_x, fixed_y - base_y, pts[2:3] - fixed_x, pts[3:4] - fixed_y], axis=0
    )


def split_pair(value):
    high = value.astype(jnp.bfloat16).astype(jnp.float32)
    return high, value - high


def pack_kernel(own_ref, mate_ref, source_ref, packed_ref):
    height, width = source_ref.shape
    half = packed_ref.shape[1]
    tile = lax.axis_index("ty")
    for part in range(width // half):
        packed_ref[part * height : (part + 1) * height, :] = source_ref[:, part * half : (part + 1) * half]
    rows = []
    for ref, owner in ((own_ref, tile), (mate_ref, tile + 1 - 2 * (tile % 2))):
        rows.extend(split_pair(local_points(ref[...], owner, width // CELL, height)))
    base = width // half * height
    packed_ref[base : base + 16, :] = jnp.concatenate(rows, axis=0).astype(jnp.bfloat16)


def main_kernel(
    strips,
    first_ref,
    count_ref,
    own_ref,
    mate_ref,
    source_ref,
    mate_source_ref,
    packed_ref,
    far_ref,
    out_ref,
    affine_ref,
    feat_ref,
    weight_ref,
    slab_ref,
    shift_ref,
    mixed_ref,
    bound_ref,
):
    height, width = source_ref.shape
    tile_len = own_ref.shape[1]
    cell_cols = width // CELL
    cell_rows = height // CELL
    groups = width // GROUP_PX
    blocks = width // LANES
    halves = blocks // 8
    tile = lax.axis_index("ty")
    odd = tile % 2
    toward = 1 - 2 * odd
    mate = tile + toward
    partner = tile - toward
    partner_mate = tile - 2 * toward
    beyond = tile + 2 * toward

    slots_from = first_ref[0] * BH - (tile - 1) * height
    slots_to = slots_from + count_ref[0] * BH
    left_half = lax.broadcasted_iota(jnp.int32, (1, LANES), 1) < LANES // 2
    pitch = slab_ref.shape[0] // (TOP_PAD + 3 * height + LOW_PAD)
    for edge in (TOP_PAD - 2, TOP_PAD - 1, TOP_PAD + 3 * height, TOP_PAD + 3 * height + 1):
        slab_ref[edge * pitch : (edge + 1) * pitch, :] = jnp.zeros((pitch, LANES), jnp.float32)

    half_cols = packed_ref.shape[1]

    def place(load, row_start, chunk):
        local = row_start + chunk * 16
        row = lax.broadcasted_iota(jnp.int32, (16, 1), 0) + local
        live = ((row >= slots_from) & (row < slots_to)).astype(jnp.float32)
        before = jnp.zeros((16, LANES), jnp.float32)
        for b in range(blocks + 1):
            if b < blocks:
                now = pltpu.roll(load(b).astype(jnp.float32) * live, LANES // 2, axis=1)
            else:
                now = jnp.zeros((16, LANES), jnp.float32)
            merged = jnp.where(left_half, before, now)
            start = (TOP_PAD + local) * pitch + b
            slab_ref[pl.ds(start, 16, stride=pitch), :] = merged
            before = now

    for chunk in range(height // 16):
        rows = slice(chunk * 16, chunk * 16 + 16)
        place(lambda b: source_ref[rows, b * LANES : (b + 1) * LANES], height, chunk)
        place(lambda b: mate_source_ref[rows, b * LANES : (b + 1) * LANES], height + toward * height, chunk)

        def from_packed(b):
            part = b * LANES // half_cols
            lane = b * LANES - part * half_cols
            return packed_ref[part * height + chunk * 16 : part * height + chunk * 16 + 16, lane : lane + LANES]

        place(from_packed, height - toward * height, chunk)

    point_rows = packed_ref[packed_ref.shape[0] - 16 :, :].astype(jnp.float32)
    far_rows = far_ref[...].astype(jnp.float32)
    sets = (
        (local_points(own_ref[...], tile, cell_cols, height), tile),
        (local_points(mate_ref[...], mate, cell_cols, height), mate),
        (point_rows[0:4] + point_rows[4:8], partner),
        (point_rows[8:12] + point_rows[12:16], partner_mate),
        (far_rows[0:4] + far_rows[4:8], beyond),
    )
    ext_row = lax.broadcasted_iota(jnp.int32, (ER, 1), 0)
    vertex_y = (fiota((ER, 1), 0) * SP + (SP / 2.0 - SP - height / 2.0)) / height
    ext_tile = tile + jnp.where(ext_row == 0, -1, jnp.where(ext_row == VR + 1, 1, 0))
    scale = float(np.sqrt(EXP2_SCALE))
    lane_px = fiota((1, LANES), 1)
    lane_px = (lax.broadcasted_iota(jnp.int32, (1, LANES), 1) // PC * CELL).astype(jnp.float32) - GROUP_PX / 2.0
    vertex_ids = lax.broadcasted_iota(jnp.int32, (NV, LANES), 0)
    point_block = lax.broadcasted_iota(jnp.int32, (NV, LANES), 1) // (LANES // CELL * PC)
    band = (jnp.abs(vertex_ids // (LANES // SP) - 1 - point_block) <= 1).astype(jnp.float32)
    vertex_scaled = (fiota((NV, 1), 0) * SP + (SP / 2.0 - LANES - GROUP_PX / 2.0)) * (scale / height)
    zero_rows = jnp.zeros((LANES - NV, weight_ref.shape[2]), jnp.bfloat16)

    totals = []
    for g in range(groups):
        weight_ref[g, NV:LANES, :] = zero_rows
        weight_ref[g, LANES + NV :, :] = zero_rows
        for s, (pts, owner) in enumerate(sets):
            usable = (jnp.abs(owner - ext_tile) <= 1) & (owner >= 0) & (owner < strips)
            usable = usable.astype(jnp.float32)
            for c in range(cell_rows):
                lanes = slice(c * cell_cols * PC + g * LANES, c * cell_cols * PC + (g + 1) * LANES)
                chunk = slice((s * cell_rows + c) * LANES, (s * cell_rows + c + 1) * LANES)
                px = (pts[0:1, lanes] + lane_px) / height
                py = (pts[1:2, lanes] + ((owner - tile) * height + c * CELL).astype(jnp.float32)) / height - 0.5
                dx = pts[2:3, lanes] / height
                dy = pts[3:4, lanes] / height
                gap_y = (py - vertex_y) * scale
                wy = jnp.exp2(-(gap_y * gap_y)) * usable
                wpx, wpy, wdx, wdy = wy * px, wy * py, wy * dx, wy * dy
                rows = (wy, wpx, wpy, wdx, wdy, wpx * px, wpx * py, wpy * py, wdx * px, wdx * py, wdy * px, wdy * py)
                for f in range(0, FEATS, 2):
                    high, low = split_pair(jnp.concatenate(rows[f : f + 2], axis=0))
                    feat_ref[g, f * ER : (f + 2) * ER, chunk] = high.astype(jnp.bfloat16)
                    feat_ref[g, NF + f * ER : NF + (f + 2) * ER, chunk] = low.astype(jnp.bfloat16)
                gap_x = px * scale - vertex_scaled
                wx = jnp.exp2(-(gap_x * gap_x)) * band
                high, low = split_pair(wx)
                weight_ref[g, 0:NV, chunk] = high.astype(jnp.bfloat16)
                weight_ref[g, LANES : LANES + NV, chunk] = low.astype(jnp.bfloat16)
        both = lax.dot_general(
            feat_ref[g], weight_ref[g], (((1,), (1,)), ((), ())), preferred_element_type=jnp.float32
        )
        both = both[:NF] + both[NF:]
        totals.append(both[:, :LANES] + both[:, LANES:])

    lane = lax.broadcasted_iota(jnp.int32, (1, LANES), 1)
    per_group = GROUP_PX // SP
    affines = []
    for h in range(halves):
        moments = None
        vertex_group = 2 * h + lane // per_group
        for g in range(groups):
            start = g * per_group - LANES // SP - h * LANES
            if start + NV <= 0 or start >= LANES:
                continue
            part = pltpu.roll(totals[g], start % LANES, axis=1)
            inside = ((lane >= start) & (lane < start + NV)).astype(jnp.float32)
            move = ((g - vertex_group) * (GROUP_PX // height)).astype(jnp.float32)
            part = [part[f * ER : (f + 1) * ER] * inside for f in range(FEATS)]
            part[5] = part[5] + move * (2.0 * part[1] + move * part[0])
            part[6] = part[6] + move * part[2]
            part[8] = part[8] + move * part[3]
            part[10] = part[10] + move * part[4]
            part[1] = part[1] + move * part[0]
            moments = part if moments is None else [x + y for x, y in zip(moments, part)]
        inverse = 1.0 / moments[0]
        mean_px, mean_py, mean_dx, mean_dy = [moments[i] * inverse for i in range(1, 5)]
        cov_xx = moments[5] * inverse - mean_px * mean_px + RIDGE_TERM
        cov_xy = moments[6] * inverse - mean_px * mean_py
        cov_yy = moments[7] * inverse - mean_py * mean_py + RIDGE_TERM
        cross_xx = moments[8] * inverse - mean_dx * mean_px - RIDGE_TERM
        cross_xy = moments[9] * inverse - mean_dx * mean_py
        cross_yx = moments[10] * inverse - mean_dy * mean_px
        cross_yy = moments[11] * inverse - mean_dy * mean_py - RIDGE_TERM
        over = 1.0 / (cov_xx * cov_yy - cov_xy * cov_xy)
        lin_xx = (cross_xx * cov_yy - cross_xy * cov_xy) * over
        lin_xy = (cross_xy * cov_xx - cross_xx * cov_xy) * over
        lin_yx = (cross_yx * cov_yy - cross_yy * cov_xy) * over
        lin_yy = (cross_yy * cov_xx - cross_yx * cov_xy) * over
        vertex_x = ((lane % per_group * SP).astype(jnp.float32) + (SP - GROUP_PX) / 2.0) / height
        delta_x = vertex_x - mean_px
        delta_y = vertex_y - mean_py
        shift_x = mean_dx + lin_xx * delta_x + lin_xy * delta_y
        shift_y = mean_dy + lin_yx * delta_x + lin_yy * delta_y
        results = (lin_xx + 1.0, lin_xy, lin_yx, lin_yy + 1.0, shift_x, shift_y)
        for i, value in enumerate(results):
            affine_ref[i, :, h * LANES : (h + 1) * LANES] = value[1 : VR + 1]
        affines.append((shift_x, shift_y))

    ext = lax.broadcasted_iota(jnp.int32, (ER, LANES), 0)
    spread = lax.broadcasted_iota(jnp.int32, (8, LANES), 0) * (LANES // SP) + lax.broadcasted_iota(jnp.int32, (8, LANES), 1) // SP
    along = (lane % SP).astype(jnp.float32) / SP - 0.5
    left_side = along < 0.0
    for comp in range(2):
        rows = []
        for h in range(halves):
            value = affines[h][comp] * float(height)
            value = jnp.where((ext == 0) & (tile == 0), jnp.broadcast_to(value[1:2], value.shape), value)
            value = jnp.where((ext == VR + 1) & (tile == strips - 1), jnp.broadcast_to(value[VR : VR + 1], value.shape), value)
            rows.append(value)
        for h in range(halves):
            value = rows[h]
            prior = rows[h - 1] if h > 0 else value
            later = rows[h + 1] if h + 1 < halves else value
            first = jnp.broadcast_to(prior[:, LANES - 1 :] if h > 0 else value[:, :1], value.shape)
            last = jnp.broadcast_to(later[:, :1] if h + 1 < halves else value[:, LANES - 1 :], value.shape)
            before = jnp.where(lane == 0, first, pltpu.roll(value, 1, axis=1))
            after = jnp.where(lane == LANES - 1, last, pltpu.roll(value, LANES - 1, axis=1))
            rise = value - before
            climb = after - value
            for e in range(VR + 2):
                at = jnp.take_along_axis(jnp.broadcast_to(value[e : e + 1], (8, LANES)), spread, axis=1)
                low = jnp.take_along_axis(jnp.broadcast_to(rise[e : e + 1], (8, LANES)), spread, axis=1)
                high = jnp.take_along_axis(jnp.broadcast_to(climb[e : e + 1], (8, LANES)), spread, axis=1)
                shift_ref[comp, e, h * 8 : (h + 1) * 8, :] = at + along * jnp.where(left_side, low, high)
            if comp == 1:
                least = jnp.min(jnp.minimum(value, jnp.minimum(before, after)), axis=1, keepdims=True)
                most = jnp.max(jnp.maximum(value, jnp.maximum(before, after)), axis=1, keepdims=True)
                for e in range(VR + 2):
                    bound_ref[0, h * ER + e] = least[e, 0]
                    bound_ref[1, h * ER + e] = most[e, 0]

    last_row = 3.0 * height
    lane_x = fiota((8, LANES), 1) + LANES / 2.0

    def bounds(e, h, row, ratio):
        at = h * ER + e
        low = row + (1.0 - ratio) * bound_ref[0, at] + ratio * bound_ref[0, at + 1]
        top = row + (1.0 - ratio) * bound_ref[1, at] + ratio * bound_ref[1, at + 1]
        low = jnp.clip(low - 0.01, -1.5, last_row + 0.5)
        top = jnp.clip(top + 0.01, -1.5, last_row + 0.5)
        low = (low + 64.0).astype(jnp.int32) - 64
        top = (top + 64.0).astype(jnp.int32) - 64
        return low, top

    def positions(e, h, row, ratio):
        blocks_of = slice(h * 8, h * 8 + 8)
        sample_x = lane_x + ((1.0 - ratio) * shift_ref[0, e, blocks_of, :] + ratio * shift_ref[0, e + 1, blocks_of, :])
        sample_y = row + ((1.0 - ratio) * shift_ref[1, e, blocks_of, :] + ratio * shift_ref[1, e + 1, blocks_of, :])
        return sample_x, sample_y

    def render(e, h, row, ratio, start):
        sample_x, sample_y = positions(e, h, row, ratio)
        floor_x = jnp.floor(sample_x)
        floor_y = jnp.floor(sample_y)
        part_x = sample_x - floor_x
        part_y = sample_y - floor_y
        floor_y = jnp.clip(floor_y, -2.0, last_row)
        floor_x = jnp.clip(floor_x, -2.0, 2.0 * LANES)
        weight_0 = jnp.where((floor_x >= 0.0) & (floor_x < 2.0 * LANES), 1.0 - part_x, 0.0)
        weight_1 = jnp.where((floor_x >= -1.0) & (floor_x < 2.0 * LANES - 1.0), part_x, 0.0)
        index = floor_x.astype(jnp.int32)
        index_0 = index & (LANES - 1)
        index_1 = (index + 1) & (LANES - 1)
        in_0 = floor_x < float(LANES)
        in_1 = floor_x < float(LANES - 1)
        step = floor_y.astype(jnp.int32) - start
        zero = jnp.zeros((8, LANES), jnp.float32)
        top_0 = top_1 = low_0 = low_1 = zero
        before = step == -1
        for j in range(TAPS):
            at = (start + (TOP_PAD + j)) * pitch + h * 8
            near = slab_ref[pl.ds(at, 8), :]
            next_one = slab_ref[pl.ds(at + 1, 8), :]
            value_0 = jnp.where(
                in_0, jnp.take_along_axis(near, index_0, axis=1), jnp.take_along_axis(next_one, index_0, axis=1)
            )
            value_1 = jnp.where(
                in_1, jnp.take_along_axis(near, index_1, axis=1), jnp.take_along_axis(next_one, index_1, axis=1)
            )
            here = step == j
            top_0 = jnp.where(here, value_0, top_0)
            top_1 = jnp.where(here, value_1, top_1)
            low_0 = jnp.where(before, value_0, low_0)
            low_1 = jnp.where(before, value_1, low_1)
            before = here
        upper = weight_0 * top_0 + weight_1 * top_1
        lower = weight_0 * low_0 + weight_1 * low_1
        return upper + part_y * (lower - upper)

    def each(q, todo):
        e = (q + 1) // 2
        for s in range(4):
            row = q * 4 + s
            ratio = (row - SP * e + SP // 2).astype(jnp.float32) * (1.0 / SP)
            for h in range(halves):
                todo(e, h, row, row.astype(jnp.float32) + float(height), ratio)

    def main_body(q, carry):
        most = jnp.int32(0)

        def todo(e, h, row, place_y, ratio):
            nonlocal most
            low, top = bounds(e, h, place_y, ratio)
            mixed_ref[pl.ds(row * blocks + h * 8, 8), :] = render(e, h, place_y, ratio, low)
            most = jnp.maximum(most, top - low)

        each(q, todo)
        bound_ref[2, q] = most.astype(jnp.float32)
        return carry

    lax.fori_loop(0, height // 4, main_body, 0)

    def rest_body(q, carry):
        @pl.when(bound_ref[2, q] > TAPS - 2.0)
        def _():
            def todo(e, h, row, place_y, ratio):
                low, top = bounds(e, h, place_y, ratio)

                def more(i, c):
                    at = pl.ds(row * blocks + h * 8, 8)
                    mixed_ref[at, :] = mixed_ref[at, :] + render(e, h, place_y, ratio, low + i * TAPS)
                    return c

                lax.fori_loop(1, (top - low + 1 + TAPS) // TAPS, more, 0)

            each(q, todo)

        return carry

    lax.fori_loop(0, height // 4, rest_body, 0)

    for part in range(height // 16):
        for b in range(blocks):
            value = mixed_ref[pl.ds(part * 16 * blocks + b, 16, stride=blocks), :]
            out_ref[part * 16 : part * 16 + 16, b * LANES : (b + 1) * LANES] = value.astype(jnp.bfloat16)


def per_device(points, source, slab_first, slab_count):
    strips = lax.axis_size("ty")
    height, width = source.shape
    tile_len = points.shape[1]
    blocks = width // LANES
    in_chip = [(i, i ^ 1) for i in range(strips)]
    across = []
    for i in range(1, strips - 1, 2):
        across.extend([(i, i + 1), (i + 1, i)])
    vmem = pl.BlockSpec(memory_space=pltpu.VMEM)
    smem = pl.BlockSpec(memory_space=pltpu.SMEM)
    mate_points = lax.ppermute(points, "ty", in_chip)
    packed_rows = width // tile_len * height + 16
    packed = pl.pallas_call(
        pack_kernel,
        out_shape=jax.ShapeDtypeStruct((packed_rows, tile_len), jnp.bfloat16),
        in_specs=[vmem] * 3,
        out_specs=vmem,
    )(points, mate_points, source)
    arrived = lax.ppermute(packed, "ty", across)
    mate_source = lax.ppermute(source, "ty", in_chip)
    far = lax.ppermute(arrived[packed_rows - 16 : packed_rows - 8], "ty", in_chip)
    groups = width // GROUP_PX
    points_axis = 5 * tile_len // groups
    pitch = (blocks + 1 + 7) // 8 * 8
    return pl.pallas_call(
        functools.partial(main_kernel, strips),
        out_shape=(
            jax.ShapeDtypeStruct((height, width), jnp.bfloat16),
            jax.ShapeDtypeStruct((6, VR, width // SP), jnp.float32),
        ),
        in_specs=[smem, smem] + [vmem] * 6,
        out_specs=(vmem, vmem),
        scratch_shapes=[
            pltpu.VMEM((groups, 2 * NF, points_axis), jnp.bfloat16),
            pltpu.VMEM((groups, 2 * LANES, points_axis), jnp.bfloat16),
            pltpu.VMEM(((TOP_PAD + 3 * height + LOW_PAD) * pitch, LANES), jnp.float32),
            pltpu.VMEM((2, VR + 2, blocks, LANES), jnp.float32),
            pltpu.VMEM((height * blocks, LANES), jnp.float32),
            pltpu.SMEM((3, 2 * ER), jnp.float32),
        ],
        compiler_params=pltpu.CompilerParams(vmem_limit_bytes=32 * 1024 * 1024),
    )(slab_first, slab_count, points, mate_points, source, mate_source, arrived, far)


def solution(mesh):
    return jax.shard_map(
        per_device,
        mesh=mesh,
        in_specs=(
            P(None, ("sec", "ty")),
            P(("sec", "ty"), None),
            P(("sec", "ty")),
            P(("sec", "ty")),
        ),
        out_specs=(P(("sec", "ty"), None), P(None, ("sec", "ty"), None)),
        check_vma=False,
    )
```

time: 90.3 us -> 32.4 us (0.36)
  the two profiles are of different devices: /device:TPU:7 before, /device:TPU:6 now
where the time goes in v1:
time: 32.4 us; the launch traced here: 31.8 us
  Pallas kernels  19 us (59%)
  waiting for transfers between devices  6.33 us (20%)
  starting transfers between devices  3.83 us (12%)
  between operations  2 us (6%)
  local copies, waits for them, and re-layouts  0.62 us (2%)
    pallas_call x1, Pallas kernels, per_device(): pl.pallas_call(functools.partial(main_kernel, strips), out_shape=(jax.Sha...  17.4 us
    ppermute x1, waiting for transfers between devices, per_device(): arrived = lax.ppermute(packed, 'ty', across)  4.95 us
    ppermute x1, starting transfers between devices, per_device(): arrived = lax.ppermute(packed, 'ty', across)  2.33 us
    pallas_call x1, Pallas kernels, per_device(): pl.pallas_call(pack_kernel, out_shape=jax.ShapeDtypeStruct((packed_rows,...  1.65 us
    ppermute x1, starting transfers between devices, per_device(): mate_source = lax.ppermute(source, 'ty', in_chip)  1.42 us
    ppermute x1, waiting for transfers between devices, per_device(): mate_points = lax.ppermute(points, 'ty', in_chip)  1.38 us
  transfers between devices with their start and end apart: 4, of which 2 were waited for; matrix products, arithmetic and copies ran while one was open for 0% of the time, Pallas kernels for 0%

profile of v1, /device:TPU:6, one launch (start us, length us, event | category | flops | bytes accessed | tf_op | source)
XLA Modules:
  0.0 31.8 jit_solution(16760845127819615136)
XLA Ops:
  0.6 0.0 copy-start
  0.6 0.1 collective-permute-start
  0.7 1.4 %collective-permute-done.mate_ref = f32[4,1024]{1,0:T(4,128)S(1)} collective-permute-done((f32[4,1024]{1,0:T(4,128)}, f32[4,1024]{1,0:T(4,128)S(1)}, u32[]{:S(2)}, u32[]{:S(2)}) %collective-permute-start) | collective-permute-done | bytes 16416 | tf_op jit(solution)/shard_map/ppermute | solution.py:380
  2.1 0.0 copy-start.2
  2.1 0.6 %copy-done.2 = f32[4,1024]{1,0:T(4,128)} copy-done((f32[4,1024]{1,0:T(4,128)}, f32[4,1024]{1,0:T(4,128)S(1)}, u32[]{:S(2)}) %copy-start.2) | copy-done | bytes 16408
  2.7 1.7 %shard_map.59 = bf16[80,1024]{1,0:T(8,128)(2,1)} custom-call(f32[4,1024]{1,0:T(4,128)} %own_ref.3, f32[4,1024]{1,0:T(4,128)} %copy-done.2, bf16[32,2048]{1,0:T(8,128)(2,1)} %source_ref.3), custom_call_target="tpu_custom_call" | custom-call | tf_op jit(solution)/shard_map/pallas_call | solution.py:382
  4.4 0.0 copy-start.1
  4.4 0.0 copy-start.3
  4.4 2.3 %collective-permute-start.2 = (bf16[80,1024]{1,0:T(8,128)(2,1)}, bf16[80,1024]{1,0:T(8,128)(2,1)S(1)}, u32[]{:S(2)}, u32[]{:S(2)}) collective-permute-start(bf16[80,1024]{1,0:T(8,128)(2,1)} %shard_map.59), channel_id=1, source_target_pairs={{1,2},{2,1},{3,4},{4,3},{5,6},{6,5},{7,8},{8,7},{9,10},{10,9},{11,... | collective-permute-start | bytes 491528 | tf_op jit(solution)/shard_map/ppermute | solution.py:388
  6.7 0.0 copy-done
  6.7 1.4 %collective-permute-start.1 = (bf16[32,2048]{1,0:T(8,128)(2,1)S(1)}, bf16[32,2048]{1,0:T(8,128)(2,1)S(1)}, u32[]{:S(2)}, u32[]{:S(2)}) collective-permute-start(bf16[32,2048]{1,0:T(8,128)(2,1)S(1)} %copy-done), channel_id=1, source_target_pairs={{0,1},{1,0},{2,3},{3,2},{4,5},{5,4},{6,7},{7,6},{8,9},{9,8},{10,11... | collective-permute-start | bytes 393224 | tf_op jit(solution)/shard_map/ppermute | solution.py:389
  8.1 4.9 %collective-permute-done.2.packed_ref = bf16[80,1024]{1,0:T(8,128)(2,1)S(1)} collective-permute-done((bf16[80,1024]{1,0:T(8,128)(2,1)}, bf16[80,1024]{1,0:T(8,128)(2,1)S(1)}, u32[]{:S(2)}, u32[]{:S(2)}) %collective-permute-start.2) | collective-permute-done | bytes 163872 | tf_op jit(solution)/shard_map/ppermute | solution.py:388
  13.1 0.0 collective-permute-start.3
  14.4 0.0 collective-permute-done.1.mate_source_ref
  14.4 0.0 collective-permute-done.3.far_ref
  14.4 0.0 copy-done.1
  14.4 0.0 copy-done.3
  14.4 17.4 %shard_map.60 = (bf16[32,2048]{1,0:T(8,128)(2,1)}, f32[6,4,256]{2,1,0:T(4,128)}) custom-call(s32[1]{0:T(128)S(6)} %copy.6.first_ref, s32[1]{0:T(128)S(6)} %copy.7.count_ref, f32[4,1024]{1,0:T(4,128)S(1)} %copy-done.1, f32[4,1024]{1,0:T(4,128)S(1)} %copy-done.3, bf16[32,2048]{1,0:T(8,128)(2,1)S(1)} %copy-done, ...), custom_call_target="tpu_custom_call" | custom-call | tf_op jit(solution)/shard_map/pallas_call | solution.py:394
  (1 shorter events, 0.0 us)
Async XLA Ops:
  0.6 6.1 %copy-start = (bf16[32,2048]{1,0:T(8,128)(2,1)S(1)}, bf16[32,2048]{1,0:T(8,128)(2,1)}, u32[]{:S(2)}) copy-start(bf16[32,2048]{1,0:T(8,128)(2,1)} %source_ref.3) | copy-start | bytes 393220
  0.6 1.5 %collective-permute-start = (f32[4,1024]{1,0:T(4,128)}, f32[4,1024]{1,0:T(4,128)S(1)}, u32[]{:S(2)}, u32[]{:S(2)}) collective-permute-start(f32[4,1024]{1,0:T(4,128)} %own_ref.3), channel_id=1, source_target_pairs={{0,1},{1,0},{2,3},{3,2},{4,5},{5,4},{6,7},{7,6},{8,9},{9,8},{10,11... | collective-permute-start | bytes 49160 | tf_op jit(solution)/shard_map/ppermute | solution.py:380
  2.1 0.6 %copy-start.2 = (f32[4,1024]{1,0:T(4,128)}, f32[4,1024]{1,0:T(4,128)S(1)}, u32[]{:S(2)}) copy-start(f32[4,1024]{1,0:T(4,128)S(1)} %collective-permute-done.mate_ref) | copy-start | bytes 49156
  4.4 10.1 %copy-start.1 = (f32[4,1024]{1,0:T(4,128)S(1)}, f32[4,1024]{1,0:T(4,128)}, u32[]{:S(2)}) copy-start(f32[4,1024]{1,0:T(4,128)} %own_ref.3) | copy-start | bytes 49156
  4.4 10.1 %copy-start.3 = (f32[4,1024]{1,0:T(4,128)S(1)}, f32[4,1024]{1,0:T(4,128)}, u32[]{:S(2)}) copy-start(f32[4,1024]{1,0:T(4,128)} %copy-done.2) | copy-start | bytes 49156
  4.4 8.7 %collective-permute-start.2 = (bf16[80,1024]{1,0:T(8,128)(2,1)}, bf16[80,1024]{1,0:T(8,128)(2,1)S(1)}, u32[]{:S(2)}, u32[]{:S(2)}) collective-permute-start(bf16[80,1024]{1,0:T(8,128)(2,1)} %shard_map.59), channel_id=1, source_target_pairs={{1,2},{2,1},{3,4},{4,3},{5,6},{6,5},{7,8},{8,7},{9,10},{10,9},{11,... | collective-permute-start | bytes 491528 | tf_op jit(solution)/shard_map/ppermute | solution.py:388
  6.7 7.7 %collective-permute-start.1 = (bf16[32,2048]{1,0:T(8,128)(2,1)S(1)}, bf16[32,2048]{1,0:T(8,128)(2,1)S(1)}, u32[]{:S(2)}, u32[]{:S(2)}) collective-permute-start(bf16[32,2048]{1,0:T(8,128)(2,1)S(1)} %copy-done), channel_id=1, source_target_pairs={{0,1},{1,0},{2,3},{3,2},{4,5},{5,4},{6,7},{7,6},{8,9},{9,8},{10,11... | collective-permute-start | bytes 393224 | tf_op jit(solution)/shard_map/ppermute | solution.py:389
  13.1 1.3 %collective-permute-start.3 = (bf16[8,1024]{1,0:T(8,128)(2,1)S(1)}, bf16[8,1024]{1,0:T(8,128)(2,1)S(1)}, u32[]{:S(2)}, u32[]{:S(2)}) collective-permute-start(bf16[8,1024]{1,0:T(8,128)(2,1)S(1)} %slice.4), channel_id=1, source_target_pairs={{0,1},{1,0},{2,3},{3,2},{4,5},{5,4},{6,7},{7,6},{8,9},{9,8},{10,11... | collective-permute-start | bytes 49160 | tf_op jit(solution)/shard_map/ppermute | solution.py:390

commit v2 on v1

--- a/solution.py
+++ b/solution.py
@@ -22,8 +22,6 @@
 NV = GROUP_PX // SP + 2 * LANES // SP
 EXP2_SCALE = 2.0 * float(np.log2(np.e))
 TAPS = 8
-TOP_PAD = 8
-LOW_PAD = 16
 
 
 def fiota(shape, dim):
@@ -74,9 +72,10 @@
     feat_ref,
     weight_ref,
     slab_ref,
-    shift_ref,
+    sample_ref,
+    base_ref,
+    span_ref,
     mixed_ref,
-    bound_ref,
 ):
     height, width = source_ref.shape
     tile_len = own_ref.shape[1]
@@ -96,11 +95,8 @@
     slots_from = first_ref[0] * BH - (tile - 1) * height
     slots_to = slots_from + count_ref[0] * BH
     left_half = lax.broadcasted_iota(jnp.int32, (1, LANES), 1) < LANES // 2
-    pitch = slab_ref.shape[0] // (TOP_PAD + 3 * height + LOW_PAD)
-    for edge in (TOP_PAD - 2, TOP_PAD - 1, TOP_PAD + 3 * height, TOP_PAD + 3 * height + 1):
-        slab_ref[edge * pitch : (edge + 1) * pitch, :] = jnp.zeros((pitch, LANES), jnp.float32)
-
     half_cols = packed_ref.shape[1]
+    slab_ref[3 * height :, :] = jnp.zeros((slab_ref.shape[0] - 3 * height, slab_ref.shape[1]), jnp.bfloat16)
 
     def place(load, row_start, chunk):
         local = row_start + chunk * 16
@@ -112,9 +108,8 @@
                 now = pltpu.roll(load(b).astype(jnp.float32) * live, LANES // 2, axis=1)
             else:
                 now = jnp.zeros((16, LANES), jnp.float32)
-            merged = jnp.where(left_half, before, now)
-            start = (TOP_PAD + local) * pitch + b
-            slab_ref[pl.ds(start, 16, stride=pitch), :] = merged
+            merged = jnp.where(left_half, before, now).astype(jnp.bfloat16)
+            slab_ref[pl.ds(pl.multiple_of(local, 16), 16), b * LANES : (b + 1) * LANES] = merged
             before = now
 
     for chunk in range(height // 16):
@@ -228,9 +223,9 @@
         affines.append((shift_x, shift_y))
 
     ext = lax.broadcasted_iota(jnp.int32, (ER, LANES), 0)
-    spread = lax.broadcasted_iota(jnp.int32, (8, LANES), 0) * (LANES // SP) + lax.broadcasted_iota(jnp.int32, (8, LANES), 1) // SP
     along = (lane % SP).astype(jnp.float32) / SP - 0.5
     left_side = along < 0.0
+    vertex_rows = []
     for comp in range(2):
         rows = []
         for h in range(halves):
@@ -238,54 +233,43 @@
             value = jnp.where((ext == 0) & (tile == 0), jnp.broadcast_to(value[1:2], value.shape), value)
             value = jnp.where((ext == VR + 1) & (tile == strips - 1), jnp.broadcast_to(value[VR : VR + 1], value.shape), value)
             rows.append(value)
+        steps = []
         for h in range(halves):
             value = rows[h]
-            prior = rows[h - 1] if h > 0 else value
-            later = rows[h + 1] if h + 1 < halves else value
-            first = jnp.broadcast_to(prior[:, LANES - 1 :] if h > 0 else value[:, :1], value.shape)
-            last = jnp.broadcast_to(later[:, :1] if h + 1 < halves else value[:, LANES - 1 :], value.shape)
+            first = jnp.broadcast_to(rows[h - 1][:, LANES - 1 :] if h > 0 else value[:, :1], value.shape)
+            last = jnp.broadcast_to(rows[h + 1][:, :1] if h + 1 < halves else value[:, LANES - 1 :], value.shape)
             before = jnp.where(lane == 0, first, pltpu.roll(value, 1, axis=1))
             after = jnp.where(lane == LANES - 1, last, pltpu.roll(value, LANES - 1, axis=1))
-            rise = value - before
-            climb = after - value
-            for e in range(VR + 2):
-                at = jnp.take_along_axis(jnp.broadcast_to(value[e : e + 1], (8, LANES)), spread, axis=1)
-                low = jnp.take_along_axis(jnp.broadcast_to(rise[e : e + 1], (8, LANES)), spread, axis=1)
-                high = jnp.take_along_axis(jnp.broadcast_to(climb[e : e + 1], (8, LANES)), spread, axis=1)
-                shift_ref[comp, e, h * 8 : (h + 1) * 8, :] = at + along * jnp.where(left_side, low, high)
-            if comp == 1:
-                least = jnp.min(jnp.minimum(value, jnp.minimum(before, after)), axis=1, keepdims=True)
-                most = jnp.max(jnp.maximum(value, jnp.maximum(before, after)), axis=1, keepdims=True)
-                for e in range(VR + 2):
-                    bound_ref[0, h * ER + e] = least[e, 0]
-                    bound_ref[1, h * ER + e] = most[e, 0]
-
+            steps.append((value, value - before, after - value))
+        vertex_rows.append(steps)
+
+    sub = lax.broadcasted_iota(jnp.int32, (8, LANES), 0).astype(jnp.float32)
+    lane_full = fiota((8, LANES), 1)
+    tents = (
+        jnp.maximum(0.0, 0.5 - sub / SP),
+        1.0 - jnp.abs(sub - SP / 2.0) / SP,
+        jnp.maximum(0.0, sub / SP - 0.5),
+    )
     last_row = 3.0 * height
-    lane_x = fiota((8, LANES), 1) + LANES / 2.0
-
-    def bounds(e, h, row, ratio):
-        at = h * ER + e
-        low = row + (1.0 - ratio) * bound_ref[0, at] + ratio * bound_ref[0, at + 1]
-        top = row + (1.0 - ratio) * bound_ref[1, at] + ratio * bound_ref[1, at + 1]
-        low = jnp.clip(low - 0.01, -1.5, last_row + 0.5)
-        top = jnp.clip(top + 0.01, -1.5, last_row + 0.5)
-        low = (low + 64.0).astype(jnp.int32) - 64
-        top = (top + 64.0).astype(jnp.int32) - 64
-        return low, top
-
-    def positions(e, h, row, ratio):
-        blocks_of = slice(h * 8, h * 8 + 8)
-        sample_x = lane_x + ((1.0 - ratio) * shift_ref[0, e, blocks_of, :] + ratio * shift_ref[0, e + 1, blocks_of, :])
-        sample_y = row + ((1.0 - ratio) * shift_ref[1, e, blocks_of, :] + ratio * shift_ref[1, e + 1, blocks_of, :])
-        return sample_x, sample_y
-
-    def render(e, h, row, ratio, start):
-        sample_x, sample_y = positions(e, h, row, ratio)
+    spans = None
+
+    def clipped_floor(sample_y):
+        return jnp.clip(jnp.floor(sample_y), -2.0, last_row)
+
+    def one_hot(base, k, offset):
+        return jnp.where(lane_full - base == float(offset), 1.0, 0.0)
+
+    def tap_rows(bases, offset, slab):
+        picks = [
+            jnp.concatenate([one_hot(bases[k], k, offset + j) for k in range(len(bases))], axis=0).astype(jnp.bfloat16)
+            for j in range(TAPS)
+        ]
+        return jnp.dot(jnp.concatenate(picks, axis=0), slab, preferred_element_type=jnp.float32)
+
+    def render(sample_x, sample_y, base, taken, k, count, offset):
         floor_x = jnp.floor(sample_x)
-        floor_y = jnp.floor(sample_y)
         part_x = sample_x - floor_x
-        part_y = sample_y - floor_y
-        floor_y = jnp.clip(floor_y, -2.0, last_row)
+        part_y = sample_y - jnp.floor(sample_y)
         floor_x = jnp.clip(floor_x, -2.0, 2.0 * LANES)
         weight_0 = jnp.where((floor_x >= 0.0) & (floor_x < 2.0 * LANES), 1.0 - part_x, 0.0)
         weight_1 = jnp.where((floor_x >= -1.0) & (floor_x < 2.0 * LANES - 1.0), part_x, 0.0)
@@ -294,21 +278,18 @@
         index_1 = (index + 1) & (LANES - 1)
         in_0 = floor_x < float(LANES)
         in_1 = floor_x < float(LANES - 1)
-        step = floor_y.astype(jnp.int32) - start
-        zero = jnp.zeros((8, LANES), jnp.float32)
-        top_0 = top_1 = low_0 = low_1 = zero
-        before = step == -1
+        step = clipped_floor(sample_y) - base
+        at = [slice((j * count + k) * 8, (j * count + k) * 8 + 8) for j in range(TAPS)]
+        near_0 = [jnp.take_along_axis(taken[i, :LANES], index_0, axis=1) for i in at]
+        next_0 = [jnp.take_along_axis(taken[i, LANES:], index_0, axis=1) for i in at]
+        near_1 = [jnp.take_along_axis(taken[i, :LANES], index_1, axis=1) for i in at]
+        next_1 = [jnp.take_along_axis(taken[i, LANES:], index_1, axis=1) for i in at]
+        top_0 = top_1 = low_0 = low_1 = jnp.zeros((8, LANES), jnp.float32)
+        before = step == float(offset - 1)
         for j in range(TAPS):
-            at = (start + (TOP_PAD + j)) * pitch + h * 8
-            near = slab_ref[pl.ds(at, 8), :]
-            next_one = slab_ref[pl.ds(at + 1, 8), :]
-            value_0 = jnp.where(
-                in_0, jnp.take_along_axis(near, index_0, axis=1), jnp.take_along_axis(next_one, index_0, axis=1)
-            )
-            value_1 = jnp.where(
-                in_1, jnp.take_along_axis(near, index_1, axis=1), jnp.take_along_axis(next_one, index_1, axis=1)
-            )
-            here = step == j
+            value_0 = jnp.where(in_0, near_0[j], next_0[j])
+            value_1 = jnp.where(in_1, near_1[j], next_1[j])
+            here = step == float(offset + j)
             top_0 = jnp.where(here, value_0, top_0)
             top_1 = jnp.where(here, value_1, top_1)
             low_0 = jnp.where(before, value_0, low_0)
@@ -318,52 +299,79 @@
         lower = weight_0 * low_0 + weight_1 * low_1
         return upper + part_y * (lower - upper)
 
-    def each(q, todo):
-        e = (q + 1) // 2
-        for s in range(4):
-            row = q * 4 + s
-            ratio = (row - SP * e + SP // 2).astype(jnp.float32) * (1.0 / SP)
-            for h in range(halves):
-                todo(e, h, row, row.astype(jnp.float32) + float(height), ratio)
-
-    def main_body(q, carry):
-        most = jnp.int32(0)
-
-        def todo(e, h, row, place_y, ratio):
-            nonlocal most
-            low, top = bounds(e, h, place_y, ratio)
-            mixed_ref[pl.ds(row * blocks + h * 8, 8), :] = render(e, h, place_y, ratio, low)
-            most = jnp.maximum(most, top - low)
-
-        each(q, todo)
-        bound_ref[2, q] = most.astype(jnp.float32)
-        return carry
-
-    lax.fori_loop(0, height // 4, main_body, 0)
-
-    def rest_body(q, carry):
-        @pl.when(bound_ref[2, q] > TAPS - 2.0)
-        def _():
-            def todo(e, h, row, place_y, ratio):
-                low, top = bounds(e, h, place_y, ratio)
+    row_groups = height // 8
+    block_spans = []
+    for b in range(blocks):
+        spread = (b % 8) * (LANES // SP) + lax.broadcasted_iota(jnp.int32, (8, LANES), 1) // SP
+        expanded = []
+        for comp in range(2):
+            value, rise, climb = vertex_rows[comp][b // 8]
+            at = jnp.take_along_axis(value, spread, axis=1)
+            low = jnp.take_along_axis(rise, spread, axis=1)
+            high = jnp.take_along_axis(climb, spread, axis=1)
+            expanded.append(at + along * jnp.where(left_side, low, high))
+        columns = slice(b * LANES, (b + 1) * LANES)
+        span = None
+        for k in range(row_groups):
+            moved = [
+                tents[0] * ex[k : k + 1] + tents[1] * ex[k + 1 : k + 2] + tents[2] * ex[k + 2 : k + 3] for ex in expanded
+            ]
+            sample_x = lane_full + (moved[0] + LANES / 2.0)
+            sample_y = sub + (moved[1] + float(k * 8 + height))
+            rows = slice(k * 8, k * 8 + 8)
+            sample_ref[0, rows, columns] = sample_x
+            sample_ref[1, rows, columns] = sample_y
+            floor_y = clipped_floor(sample_y)
+            base = jnp.min(floor_y, axis=1, keepdims=True)
+            base_ref[b, rows, :] = jnp.broadcast_to(base, (8, LANES))
+            span = floor_y - base if span is None else jnp.maximum(span, floor_y - base)
+        span_ref[b] = span
+        spans = span if spans is None else jnp.maximum(spans, span)
+
+    for b in range(blocks):
+        columns = slice(b * LANES, (b + 1) * LANES)
+        bases = [base_ref[b, k * 8 : k * 8 + 8, :] for k in range(row_groups)]
+        taken = tap_rows(bases, 0, slab_ref[:, b * LANES : (b + 2) * LANES])
+        for k in range(row_groups):
+            rows = slice(k * 8, k * 8 + 8)
+            mixed_ref[rows, columns] = render(
+                sample_ref[0, rows, columns], sample_ref[1, rows, columns], bases[k], taken, k, row_groups, 0
+            )
+
+    @pl.when(jnp.max(spans) > TAPS - 2.0)
+    def _():
+        def rest(b, carry):
+            widest = jnp.max(span_ref[b])
+
+            @pl.when(widest > TAPS - 2.0)
+            def _():
+                start = pl.multiple_of(b * LANES, LANES)
+                columns = pl.ds(start, LANES)
+                bases = [base_ref[b, k * 8 : k * 8 + 8, :] for k in range(row_groups)]
 
                 def more(i, c):
-                    at = pl.ds(row * blocks + h * 8, 8)
-                    mixed_ref[at, :] = mixed_ref[at, :] + render(e, h, place_y, ratio, low + i * TAPS)
+                    moved_bases = [base + (i * TAPS).astype(jnp.float32) for base in bases]
+                    taken = tap_rows(moved_bases, 0, slab_ref[:, pl.ds(start, 2 * LANES)])
+                    for k in range(row_groups):
+                        rows = slice(k * 8, k * 8 + 8)
+                        mixed_ref[rows, columns] = mixed_ref[rows, columns] + render(
+                            sample_ref[0, rows, columns],
+                            sample_ref[1, rows, columns],
+                            moved_bases[k],
+                            taken,
+                            k,
+                            row_groups,
+                            0,
+                        )
                     return c
 
-                lax.fori_loop(1, (top - low + 1 + TAPS) // TAPS, more, 0)
-
-            each(q, todo)
-
-        return carry
-
-    lax.fori_loop(0, height // 4, rest_body, 0)
-
-    for part in range(height // 16):
-        for b in range(blocks):
-            value = mixed_ref[pl.ds(part * 16 * blocks + b, 16, stride=blocks), :]
-            out_ref[part * 16 : part * 16 + 16, b * LANES : (b + 1) * LANES] = value.astype(jnp.bfloat16)
+                lax.fori_loop(1, (widest.astype(jnp.int32) + 1 + TAPS) // TAPS, more, 0)
+
+            return carry
+
+        lax.fori_loop(0, blocks, rest, 0)
+
+    out_ref[...] = mixed_ref[...].astype(jnp.bfloat16)
 
 
 def per_device(points, source, slab_first, slab_count):
@@ -390,7 +398,6 @@
     far = lax.ppermute(arrived[packed_rows - 16 : packed_rows - 8], "ty", in_chip)
     groups = width // GROUP_PX
     points_axis = 5 * tile_len // groups
-    pitch = (blocks + 1 + 7) // 8 * 8
     return pl.pallas_call(
         functools.partial(main_kernel, strips),
         out_shape=(
@@ -402,10 +409,11 @@
         scratch_shapes=[
             pltpu.VMEM((groups, 2 * NF, points_axis), jnp.bfloat16),
             pltpu.VMEM((groups, 2 * LANES, points_axis), jnp.bfloat16),
-            pltpu.VMEM(((TOP_PAD + 3 * height + LOW_PAD) * pitch, LANES), jnp.float32),
-            pltpu.VMEM((2, VR + 2, blocks, LANES), jnp.float32),
-            pltpu.VMEM((height * blocks, LANES), jnp.float32),
-            pltpu.SMEM((3, 2 * ER), jnp.float32),
+            pltpu.VMEM((LANES, width + LANES), jnp.bfloat16),
+            pltpu.VMEM((2, height, width), jnp.float32),
+            pltpu.VMEM((blocks, height, LANES), jnp.float32),
+            pltpu.VMEM((blocks, 8, LANES), jnp.float32),
+            pltpu.VMEM((height, width), jnp.float32),
         ],
         compiler_params=pltpu.CompilerParams(vmem_limit_bytes=32 * 1024 * 1024),
     )(slab_first, slab_count, points, mate_points, source, mate_source, arrived, far)

time: 32.4 us -> 24.9 us (0.77)
  the two profiles are of different devices: /device:TPU:6 before, /device:TPU:0 now
where the time goes in v2:
time: 24.9 us; the launch traced here: 24.6 us
  Pallas kernels  11.1 us (45%)
  starting transfers between devices  9.82 us (39%)
  between operations  1.99 us (8%)
  waiting for transfers between devices  1.06 us (4%)
  local copies, waits for them, and re-layouts  0.62 us (2%)
    pallas_call x1, Pallas kernels, per_device(): pl.pallas_call(functools.partial(main_kernel, strips), out_shape=(jax.Sha...  9.49 us
    ppermute x1, starting transfers between devices, per_device(): far = lax.ppermute(arrived[packed_rows - 16:packed_rows - 8], 'ty', in_chip)  4.27 us
    ppermute x1, starting transfers between devices, per_device(): mate_source = lax.ppermute(source, 'ty', in_chip)  4.25 us
    pallas_call x1, Pallas kernels, per_device(): pl.pallas_call(pack_kernel, out_shape=jax.ShapeDtypeStruct((packed_rows,...  1.65 us
    ppermute x1, waiting for transfers between devices, per_device(): mate_points = lax.ppermute(points, 'ty', in_chip)  1.05 us
    ppermute x1, starting transfers between devices, per_device(): arrived = lax.ppermute(packed, 'ty', across)  0.79 us
    unnamed x8, local copies, waits for them, and re-layouts  0.62 us
    ppermute x1, starting transfers between devices, per_device(): mate_points = lax.ppermute(points, 'ty', in_chip)  0.52 us
  transfers between devices with their start and end apart: 4, of which 1 were waited for; matrix products, arithmetic and copies ran while one was open for 0% of the time, Pallas kernels for 0%

profile of v2, /device:TPU:0, one launch (start us, length us, event | category | flops | bytes accessed | tf_op | source)
XLA Modules:
  0.0 24.6 jit_solution(10669195147095870041)
XLA Ops:
  0.6 0.0 copy-start
  0.6 0.5 %collective-permute-start = (f32[4,1024]{1,0:T(4,128)}, f32[4,1024]{1,0:T(4,128)S(1)}, u32[]{:S(2)}, u32[]{:S(2)}) collective-permute-start(f32[4,1024]{1,0:T(4,128)} %own_ref.3), channel_id=1, source_target_pairs={{0,1},{1,0},{2,3},{3,2},{4,5},{5,4},{6,7},{7,6},{8,9},{9,8},{10,11... | collective-permute-start | bytes 49160 | tf_op jit(solution)/shard_map/ppermute | solution.py:388
  1.2 1.0 %collective-permute-done.mate_ref = f32[4,1024]{1,0:T(4,128)S(1)} collective-permute-done((f32[4,1024]{1,0:T(4,128)}, f32[4,1024]{1,0:T(4,128)S(1)}, u32[]{:S(2)}, u32[]{:S(2)}) %collective-permute-start) | collective-permute-done | bytes 16416 | tf_op jit(solution)/shard_map/ppermute | solution.py:388
  2.2 0.0 copy-start.2
  2.2 0.6 %copy-done.2 = f32[4,1024]{1,0:T(4,128)} copy-done((f32[4,1024]{1,0:T(4,128)}, f32[4,1024]{1,0:T(4,128)S(1)}, u32[]{:S(2)}) %copy-start.2) | copy-done | bytes 16408
  2.8 1.7 %shard_map.59 = bf16[80,1024]{1,0:T(8,128)(2,1)} custom-call(f32[4,1024]{1,0:T(4,128)} %own_ref.3, f32[4,1024]{1,0:T(4,128)} %copy-done.2, bf16[32,2048]{1,0:T(8,128)(2,1)} %source_ref.3), custom_call_target="tpu_custom_call" | custom-call | tf_op jit(solution)/shard_map/pallas_call | solution.py:390
  4.5 0.0 copy-start.1
  4.5 0.0 copy-start.3
  4.5 0.8 %collective-permute-start.2 = (bf16[80,1024]{1,0:T(8,128)(2,1)}, bf16[80,1024]{1,0:T(8,128)(2,1)S(1)}, u32[]{:S(2)}, u32[]{:S(2)}) collective-permute-start(bf16[80,1024]{1,0:T(8,128)(2,1)} %shard_map.59), channel_id=1, source_target_pairs={{1,2},{2,1},{3,4},{4,3},{5,6},{6,5},{7,8},{8,7},{9,10},{10,9},{11,... | collective-permute-start | bytes 491528 | tf_op jit(solution)/shard_map/ppermute | solution.py:396
  5.3 0.0 copy-done
  5.3 4.2 %collective-permute-start.1 = (bf16[32,2048]{1,0:T(8,128)(2,1)S(1)}, bf16[32,2048]{1,0:T(8,128)(2,1)S(1)}, u32[]{:S(2)}, u32[]{:S(2)}) collective-permute-start(bf16[32,2048]{1,0:T(8,128)(2,1)S(1)} %copy-done), channel_id=1, source_target_pairs={{0,1},{1,0},{2,3},{3,2},{4,5},{5,4},{6,7},{7,6},{8,9},{9,8},{10,11... | collective-permute-start | bytes 393224 | tf_op jit(solution)/shard_map/ppermute | solution.py:397
  9.5 0.0 collective-permute-done.2.packed_ref
  9.5 4.3 %collective-permute-start.3 = (bf16[8,1024]{1,0:T(8,128)(2,1)S(1)}, bf16[8,1024]{1,0:T(8,128)(2,1)S(1)}, u32[]{:S(2)}, u32[]{:S(2)}) collective-permute-start(bf16[8,1024]{1,0:T(8,128)(2,1)S(1)} %slice.4), channel_id=1, source_target_pairs={{0,1},{1,0},{2,3},{3,2},{4,5},{5,4},{6,7},{7,6},{8,9},{9,8},{10,11... | collective-permute-start | bytes 49160 | tf_op jit(solution)/shard_map/ppermute | solution.py:398
  15.1 0.0 collective-permute-done.1.mate_source_ref
  15.1 0.0 collective-permute-done.3.far_ref
  15.1 0.0 copy-done.1
  15.1 0.0 copy-done.3
  15.1 9.5 %shard_map.60 = (bf16[32,2048]{1,0:T(8,128)(2,1)}, f32[6,4,256]{2,1,0:T(4,128)}) custom-call(s32[1]{0:T(128)S(6)} %copy.6.first_ref, s32[1]{0:T(128)S(6)} %copy.7.count_ref, f32[4,1024]{1,0:T(4,128)S(1)} %copy-done.1, f32[4,1024]{1,0:T(4,128)S(1)} %copy-done.3, bf16[32,2048]{1,0:T(8,128)(2,1)S(1)} %copy-done, ...), custom_call_target="tpu_custom_call" | custom-call | tf_op jit(solution)/shard_map/pallas_call | solution.py:401
  (1 shorter events, 0.0 us)
Async XLA Ops:
  0.6 4.6 %copy-start = (bf16[32,2048]{1,0:T(8,128)(2,1)S(1)}, bf16[32,2048]{1,0:T(8,128)(2,1)}, u32[]{:S(2)}) copy-start(bf16[32,2048]{1,0:T(8,128)(2,1)} %source_ref.3) | copy-start | bytes 393220
  0.6 1.6 %collective-permute-start = (f32[4,1024]{1,0:T(4,128)}, f32[4,1024]{1,0:T(4,128)S(1)}, u32[]{:S(2)}, u32[]{:S(2)}) collective-permute-start(f32[4,1024]{1,0:T(4,128)} %own_ref.3), channel_id=1, source_target_pairs={{0,1},{1,0},{2,3},{3,2},{4,5},{5,4},{6,7},{7,6},{8,9},{9,8},{10,11... | collective-permute-start | bytes 49160 | tf_op jit(solution)/shard_map/ppermute | solution.py:388
  2.2 0.6 %copy-start.2 = (f32[4,1024]{1,0:T(4,128)}, f32[4,1024]{1,0:T(4,128)S(1)}, u32[]{:S(2)}) copy-start(f32[4,1024]{1,0:T(4,128)S(1)} %collective-permute-done.mate_ref) | copy-start | bytes 49156
  4.5 10.7 %copy-start.1 = (f32[4,1024]{1,0:T(4,128)S(1)}, f32[4,1024]{1,0:T(4,128)}, u32[]{:S(2)}) copy-start(f32[4,1024]{1,0:T(4,128)} %own_ref.3) | copy-start | bytes 49156
  4.5 10.7 %copy-start.3 = (f32[4,1024]{1,0:T(4,128)S(1)}, f32[4,1024]{1,0:T(4,128)}, u32[]{:S(2)}) copy-start(f32[4,1024]{1,0:T(4,128)} %copy-done.2) | copy-start | bytes 49156
  4.5 5.1 %collective-permute-start.2 = (bf16[80,1024]{1,0:T(8,128)(2,1)}, bf16[80,1024]{1,0:T(8,128)(2,1)S(1)}, u32[]{:S(2)}, u32[]{:S(2)}) collective-permute-start(bf16[80,1024]{1,0:T(8,128)(2,1)} %shard_map.59), channel_id=1, source_target_pairs={{1,2},{2,1},{3,4},{4,3},{5,6},{6,5},{7,8},{8,7},{9,10},{10,9},{11,... | collective-permute-start | bytes 491528 | tf_op jit(solution)/shard_map/ppermute | solution.py:396
  5.3 9.8 %collective-permute-start.1 = (bf16[32,2048]{1,0:T(8,128)(2,1)S(1)}, bf16[32,2048]{1,0:T(8,128)(2,1)S(1)}, u32[]{:S(2)}, u32[]{:S(2)}) collective-permute-start(bf16[32,2048]{1,0:T(8,128)(2,1)S(1)} %copy-done), channel_id=1, source_target_pairs={{0,1},{1,0},{2,3},{3,2},{4,5},{5,4},{6,7},{7,6},{8,9},{9,8},{10,11... | collective-permute-start | bytes 393224 | tf_op jit(solution)/shard_map/ppermute | solution.py:397
  9.5 5.6 %collective-permute-start.3 = (bf16[8,1024]{1,0:T(8,128)(2,1)S(1)}, bf16[8,1024]{1,0:T(8,128)(2,1)S(1)}, u32[]{:S(2)}, u32[]{:S(2)}) collective-permute-start(bf16[8,1024]{1,0:T(8,128)(2,1)S(1)} %slice.4), channel_id=1, source_target_pairs={{0,1},{1,0},{2,3},{3,2},{4,5},{5,4},{6,7},{7,6},{8,9},{9,8},{10,11... | collective-permute-start | bytes 49160 | tf_op jit(solution)/shard_map/ppermute | solution.py:398
